TPU v7x, 512 devices: a whole 4x4x16 slice. The times are simulated.
512 devices in a mesh: seq: 16 (over z), row: 32 (over y, x, core).
Axes of the slice: x: 4, y: 4, z: 16, core: 2. Of those that a mesh axis runs over, the one named last changes fastest.
Arguments:
- queries: bfloat16 [3, 512, 8192], P(None, 'row'), may hold values from -128 to 128
- prefix_keys: bfloat16 [24576, 512], P('seq'), may hold values from -6 to 6
- prefix_values: bfloat16 [24576, 512], P('seq'), may hold values from -6 to 6
- suffix_keys: bfloat16 [512, 1024, 512], P('row', 'seq'), may hold values from -6 to 6
- suffix_values: bfloat16 [512, 1024, 512], P('row', 'seq'), may hold values from -6 to 6
- new_keys: bfloat16 [3, 512, 512], P(None, 'row'), may hold values from -6 to 6
- new_values: bfloat16 [3, 512, 512], P(None, 'row'), may hold values from -6 to 6
- lengths: int32 [512], P('row'), may hold values from 64 to 1024
- pair_of: int32 [512], replicated, may hold values from 0 to 511, as said below
- guidance: float32 [64], replicated, may hold values from 1 to 3
Outputs:
- guided: bfloat16 [3, 512, 8192], P(None, 'row', 'seq')
Inputs may be any that keep to these rules, and one draw needn't show every extreme that they name: pair_of[pair_of[r]] = r; a row of the first half of the 512 rows is paired with a row of the second half, and pair_of[r] // 16 = (r // 16 + 512 / 32) mod (32).
All inputs are finite; a program needn't handle non-finite values.
Results may differ from a plain program's by a relative error of at most 0.014.
Values may be sent and summed in bfloat16 or wider, within the bound.
A program may use at most 128 MiB of HBM per device.

v0:
```python
import jax
import jax.numpy as jnp
from jax import lax
from jax.sharding import PartitionSpec as P

HD = 128


def shifted(value, axis, steps):
    count = lax.axis_size(axis)
    pairs = [(source, (source + steps) % count) for source in range(count)]
    return lax.ppermute(value, axis, pairs)


def local(
    queries,
    prefix_keys,
    prefix_values,
    suffix_keys,
    suffix_values,
    new_keys,
    new_values,
    lengths,
    pair_of,
    guidance,
):
    steps, row_dev, width = queries.shape
    kv_heads = prefix_keys.shape[1] // HD
    heads = width // HD
    group = heads // kv_heads
    scale = HD ** (-0.5)
    query = queries.reshape(steps, row_dev, kv_heads, group, HD)
    pre_keys = prefix_keys.reshape(-1, kv_heads, HD)
    pre_values = prefix_values.reshape(-1, kv_heads, HD)
    suf_keys = suffix_keys.reshape(row_dev, -1, kv_heads, HD)
    suf_values = suffix_values.reshape(row_dev, -1, kv_heads, HD)
    suf_dev = suf_keys.shape[1]
    pre_scores = (
        jnp.einsum("trkgd,nkd->trkgn", query, pre_keys, preferred_element_type=jnp.float32) * scale
    )
    suf_scores = (
        jnp.einsum("trkgd,rnkd->trkgn", query, suf_keys, preferred_element_type=jnp.float32) * scale
    )
    position = lax.axis_index("seq") * suf_dev + jnp.arange(suf_dev, dtype=jnp.int32)
    live = position[None, :] < lengths[:, None]
    suf_scores = jnp.where(live[None, :, None, None, :], suf_scores, -1e30)
    top = jnp.maximum(jnp.max(pre_scores, -1), jnp.max(suf_scores, -1))
    pre_weights = jnp.exp(pre_scores - top[..., None])
    suf_weights = jnp.exp(suf_scores - top[..., None])
    total = jnp.sum(pre_weights, -1) + jnp.sum(suf_weights, -1)
    summed = jnp.einsum(
        "trkgn,nkd->trkgd",
        pre_weights.astype(jnp.bfloat16),
        pre_values,
        preferred_element_type=jnp.float32,
    )
    summed = summed + jnp.einsum(
        "trkgn,rnkd->trkgd",
        suf_weights.astype(jnp.bfloat16),
        suf_values,
        preferred_element_type=jnp.float32,
    )
    top = top.reshape(steps, row_dev, heads)
    total = total.reshape(steps, row_dev, heads)
    summed = summed.reshape(steps, row_dev, heads, HD)
    shards = lax.axis_size("seq")
    share = heads // shards
    first = lax.axis_index("seq") * share
    pieces = (
        lax.all_to_all(top[None], "seq", split_axis=3, concat_axis=0, tiled=True),
        lax.all_to_all(total[None], "seq", split_axis=3, concat_axis=0, tiled=True),
        lax.all_to_all(summed[None], "seq", split_axis=3, concat_axis=0, tiled=True),
    )
    top_own = jnp.max(pieces[0], 0)
    factor = jnp.exp(pieces[0] - top_own[None])
    total_own = jnp.sum(pieces[1] * factor, 0)
    summed_own = jnp.sum(pieces[2] * factor[..., None], 0)
    fresh_keys = new_keys.reshape(steps, row_dev, kv_heads, HD)
    fresh_values = new_values.reshape(steps, row_dev, kv_heads, HD)
    step_index = jnp.arange(steps, dtype=jnp.int32)
    causal = step_index[None, :] <= step_index[:, None]
    new_scores = (
        jnp.einsum("trkgd,jrkd->trkgj", query, fresh_keys, preferred_element_type=jnp.float32)
        * scale
    )
    new_scores = jnp.where(causal[:, None, None, None, :], new_scores, -1e30)
    new_scores = lax.dynamic_slice_in_dim(
        new_scores.reshape(steps, row_dev, heads, steps), first, share, 2
    )
    kv_index = (first + jnp.arange(share, dtype=jnp.int32)) // group
    own_values = jnp.take(fresh_values, kv_index, axis=2)
    highest = jnp.maximum(top_own, jnp.max(new_scores, -1))
    new_weights = jnp.exp(new_scores - highest[..., None])
    factor = jnp.exp(top_own - highest)
    total_own = total_own * factor + jnp.sum(new_weights, -1)
    summed_own = summed_own * factor[..., None] + jnp.einsum(
        "trhj,jrhd->trhd",
        new_weights.astype(jnp.bfloat16),
        own_values,
        preferred_element_type=jnp.float32,
    )
    attention = (summed_own / total_own[..., None]).astype(jnp.bfloat16)
    mine = lax.axis_index("row") * row_dev + jnp.arange(row_dev, dtype=jnp.int32)
    partner = jnp.take(pair_of, mine)
    across = shifted(attention, "row", lax.axis_size("row") // 2)
    other = jnp.take(across, partner % row_dev, axis=1)
    lower = (mine < partner)[None, :, None, None]
    cond = jnp.where(lower, attention, other).astype(jnp.float32)
    uncond = jnp.where(lower, other, attention).astype(jnp.float32)
    scales = lax.dynamic_slice_in_dim(guidance, first, share, 0)
    mix = uncond + scales[None, None, :, None] * (cond - uncond)
    norm = jnp.sqrt(jnp.mean(mix * mix, -1, keepdims=True) + 1e-06)
    return (mix / norm).reshape(steps, row_dev, share * HD).astype(jnp.bfloat16)


def solution(mesh):
    placed = (
        P(None, "row", None),
        P("seq", None),
        P("seq", None),
        P("row", "seq", None),
        P("row", "seq", None),
        P(None, "row", None),
        P(None, "row", None),
        P("row"),
        P(),
        P(),
    )
    return jax.shard_map(
        local, mesh=mesh, in_specs=placed, out_specs=P(None, "row", "seq"), check_vma=False
    )
```

profile of v0, /device:TPU:6, one launch (start us, length us, event | category | flops | bytes accessed | tf_op | source)
XLA Modules:
  0.0 161.6 jit_solution(14094815277994840393)
XLA Ops:
  0.0 1.4 copy.247
  1.4 0.0 copy-done.6
  1.5 1.2 reshape.313
  2.6 2.4 %reshape.311 = bf16[1536,4,128]{2,1,0:T(4,128)(2,1)S(1)} reshape(bf16[1536,512]{1,0:T(8,128)(2,1)} %param.11) | data formatting | bytes 3145728 | tf_op jit(solution)/shard_map/reshape | solution.py:33
  5.0 0.1 broadcast_compare_fusion
  5.1 7.9 %bitcast_reduce_fusion = (f32[3,16,4,16]{3,1,0,2:T(8,128)S(1)}, f32[4,1536,3,16,16]{1,4,3,2,0:T(8,128)}) fusion(bf16[3,16,4,16,128]{4,3,2,1,0:T(8,128)(2,1)S(1)} %bitcast.109, bf16[1536,4,128,1,1]{2,1,0,4,3:T(4,128)(2,1)S(1)} %bitcast.106), kind=kOutput, calls=%fused_computation.4 | convolution fusion | flops 1217393664 | bytes 21245952 | tf_op jit(solution)/shard_map/trkgd,nkd->trkgn/dot_general | solution.py:39
  13.0 0.8 bitcast_reduce_fusion.1
  13.9 0.1 copy.198
  13.9 9.6 %fusion.1 = f32[3,16,4,16]{3,1,0,2:T(8,128)S(1)} fusion(f32[4,1536,3,16,16]{1,4,3,2,0:T(8,128)} %get-tuple-element.16, f32[3,16,4,16]{3,1,0,2:T(8,128)S(1)} %copy_maximum_fusion), kind=kLoop, calls=%fused_computation.6 | loop fusion | flops 14152704 | bytes 18898944 | tf_op jit(solution)/shard_map/reduce_sum | solution.py:50
  23.6 1.4 fusion.12
  25.0 0.1 copy.242
  25.2 0.1 reshape.349
  25.3 0.5 broadcast.408
  25.8 0.9 reduce.3
  26.7 0.7 reshape.352
  27.5 15.2 %all-to-all-start.2 = ((f32[16,1,192]{2,1,0:T(1,128)}), f32[16,1,192]{2,1,0:T(1,128)}, u32[]{:S(2)}, u32[]{:S(2)}) async-start(f32[16,1,192]{2,1,0:T(1,128)} %reshape.352), calls=%async_computation.2 | async-start | bytes 32768 | tf_op jit(solution)/shard_map/all_to_all | solution.py:71
  42.7 0.4 reshape.314
  43.2 8.0 %fusion.3 = f32[4,3,16,16,128]{4,3,2,1,0:T(8,128)S(1)} fusion(f32[4,1536,3,16,16]{1,4,3,2,0:T(8,128)} %get-tuple-element.16, f32[3,16,4,16]{3,1,0,2:T(8,128)S(1)} %copy_maximum_fusion, bf16[1536,4,128,1,1]{2,1,0,4,3:T(4,128)(2,1)S(1)} %bitcast.108), kind=kOutput, calls=%fused_computation.8 | convolution fusion | flops 1222115328 | bytes 22032384 | tf_op jit(solution)/shard_map/trkgn,nkd->trkgd/dot_general | solution.py:51
  51.2 0.1 copy.239
  51.4 0.1 reshape.348
  51.5 0.9 reduce.1
  52.4 0.7 reshape.350
  53.1 1.3 reshape.315
  54.5 0.8 all-to-all-done.2
  55.3 11.2 %all-to-all-start.1 = ((f32[16,1,192]{2,1,0:T(1,128)}), f32[16,1,192]{2,1,0:T(1,128)S(1)}, u32[]{:S(2)}, u32[]{:S(2)}) async-start(f32[16,1,192]{2,1,0:T(1,128)} %reshape.350), calls=%async_computation.1 | async-start | bytes 32768 | tf_op jit(solution)/shard_map/all_to_all | solution.py:70
  66.5 0.6 bitcast_add_fusion
  67.1 0.2 copy.201
  67.3 2.1 %copy.202 = f32[1,3,16,64,128]{4,2,1,0,3:T(8,128)} copy(f32[1,3,16,64,128]{4,3,2,1,0:T(8,128)S(1)} %bitcast.107) | data formatting | bytes 3145728 | tf_op jit(solution)/shard_map/broadcast_in_dim;reshape | solution.py:72
  69.3 9.7 %all-to-all-done.1 = f32[16,1,192]{2,1,0:T(1,128)S(1)} async-done(((f32[16,1,192]{2,1,0:T(1,128)}), f32[16,1,192]{2,1,0:T(1,128)S(1)}, u32[]{:S(2)}, u32[]{:S(2)}) %all-to-all-start.1) | async-done | bytes 12320 | tf_op jit(solution)/shard_map/all_to_all | solution.py:70
  79.0 0.6 copy-done.8
  79.6 3.7 %all-to-all-start = ((f32[1,3,16,64,128]{4,2,1,0,3:T(8,128)}), f32[1,3,16,64,128]{4,2,1,0,3:T(8,128)S(1)}, u32[]{:S(2)}, u32[]{:S(2)}) async-start(f32[1,3,16,64,128]{4,2,1,0,3:T(8,128)} %copy.202), calls=%async_computation | async-start | bytes 3145728 | tf_op jit(solution)/shard_map/all_to_all | solution.py:72
  83.3 0.0 copy-start.1
  83.4 0.0 copy-done.10
  83.4 0.0 copy-start.9
  83.4 1.5 fusion.15
  84.9 0.1 copy.210
  85.0 0.2 reshape.317
  85.2 0.1 dynamic-slice_reduce_fusion
  85.3 0.1 copy.211
  85.4 0.0 copy-done
  85.4 0.6 gather_fusion.1
  86.0 0.7 gather_fusion
  86.8 0.1 select_bitcast_fusion
  86.8 1.4 reduce.4
  88.2 0.2 reshape.353
  88.5 0.7 reduce.2
  89.1 0.2 reshape.351
  89.4 0.1 copy.214
  89.5 0.1 fusion.28
  89.6 0.1 copy.222
  89.7 0.1 multiply_reduce_fusion.1
  89.7 0.0 copy-start.12
  89.8 0.4 copy.207
  90.1 0.5 copy.216
  90.7 0.2 fusion.26
  90.9 60.5 %all-to-all-done = f32[1,3,16,64,128]{4,2,1,0,3:T(8,128)S(1)} async-done(((f32[1,3,16,64,128]{4,2,1,0,3:T(8,128)}), f32[1,3,16,64,128]{4,2,1,0,3:T(8,128)S(1)}, u32[]{:S(2)}, u32[]{:S(2)}) %all-to-all-start) | async-done | bytes 1572896 | tf_op jit(solution)/shard_map/all_to_all | solution.py:72
  151.4 1.0 fusion.7
  152.4 0.1 fusion.24
  152.5 5.1 %collective-permute-start = (bf16[3,16,4,128]{3,1,2,0:T(8,128)(2,1)S(1)}, bf16[3,16,4,128]{3,1,2,0:T(8,128)(2,1)S(1)}, u32[]{:S(2)}, u32[]{:S(2)}) collective-permute-start(bf16[3,16,4,128]{3,1,2,0:T(8,128)(2,1)S(1)} %fusion.24), channel_id=1, source_target_pairs={{0,16},{1,17},{2,18},{3,19},{4,20},{5,21},{6,22},{7,23},{8,24},{9,... | collective-permute-start | bytes 147464 | tf_op jit(solution)/shard_map/ppermute | solution.py:12
  157.7 0.1 dynamic_slice.7
  157.8 2.3 %collective-permute-done = bf16[3,16,4,128]{3,1,2,0:T(8,128)(2,1)S(1)} collective-permute-done((bf16[3,16,4,128]{3,1,2,0:T(8,128)(2,1)S(1)}, bf16[3,16,4,128]{3,1,2,0:T(8,128)(2,1)S(1)}, u32[]{:S(2)}, u32[]{:S(2)}) %collective-permute-start) | collective-permute-done | bytes 49184 | tf_op jit(solution)/shard_map/ppermute | solution.py:12
  160.1 0.6 gather_fusion.2
  160.7 0.2 multiply_reduce_fusion
  160.9 0.8 copy_bitcast_fusion
  (41 shorter events, 0.4 us)
Async XLA Ops:
  0.0 85.4 %copy-start = (bf16[3,16,512]{2,1,0:T(8,128)(2,1)S(1)}, bf16[3,16,512]{2,1,0:T(8,128)(2,1)}, u32[]{:S(2)}) copy-start(bf16[3,16,512]{2,1,0:T(8,128)(2,1)} %param.16) | copy-start | bytes 147460
  0.0 1.5 copy-start.6
  1.4 11.6 %copy-start.2 = (bf16[6,8,64,128]{3,2,1,0:T(8,128)(2,1)}, bf16[6,8,64,128]{3,2,1,0:T(8,128)(2,1)S(1)}, u32[]{:S(2)}) copy-start(bf16[6,8,64,128]{3,2,1,0:T(8,128)(2,1)S(1)} %copy.247) | copy-start | bytes 2359300
  2.6 2.4 %copy-start.11 = (s32[16]{0:T(128)S(1)}, s32[16]{0:T(128)}, u32[]{:S(2)}) copy-start(s32[16]{0:T(128)} %param.17) | copy-start | bytes 196
  5.1 7.9 %copy-start.7 = (bf16[16,64,4,128]{3,2,1,0:T(4,128)(2,1)S(1)}, bf16[16,64,4,128]{3,2,1,0:T(4,128)(2,1)}, u32[]{:S(2)}) copy-start(bf16[16,64,4,128]{3,2,1,0:T(4,128)(2,1)} %reshape.313) | copy-start | bytes 3145732
  23.6 19.2 %copy-start.5 = (bf16[1536,512]{1,0:T(8,128)(2,1)S(1)}, bf16[1536,512]{1,0:T(8,128)(2,1)}, u32[]{:S(2)}) copy-start(bf16[1536,512]{1,0:T(8,128)(2,1)} %param.12) | copy-start | bytes 4718596
  27.5 27.8 %all-to-all-start.2 = ((f32[16,1,192]{2,1,0:T(1,128)}), f32[16,1,192]{2,1,0:T(1,128)}, u32[]{:S(2)}, u32[]{:S(2)}) async-start(f32[16,1,192]{2,1,0:T(1,128)} %reshape.352), calls=%async_computation.2 | async-start | bytes 32768 | tf_op jit(solution)/shard_map/all_to_all | solution.py:71
  51.2 15.3 %copy-start.4 = (bf16[3,16,4,16,64]{4,3,0,2,1:T(8,128)(2,1)S(1)}, bf16[3,16,4,16,64]{4,3,0,2,1:T(8,128)(2,1)}, u32[]{:S(2)}) copy-start(bf16[3,16,4,16,64]{4,3,0,2,1:T(8,128)(2,1)} %get-tuple-element.12) | copy-start | bytes 1179652
  55.3 23.7 %all-to-all-start.1 = ((f32[16,1,192]{2,1,0:T(1,128)}), f32[16,1,192]{2,1,0:T(1,128)S(1)}, u32[]{:S(2)}, u32[]{:S(2)}) async-start(f32[16,1,192]{2,1,0:T(1,128)} %reshape.350), calls=%async_computation.1 | async-start | bytes 32768 | tf_op jit(solution)/shard_map/all_to_all | solution.py:70
  69.3 14.0 %copy-start.10 = (bf16[3,16,512]{2,1,0:T(8,128)(2,1)S(1)}, bf16[3,16,512]{2,1,0:T(8,128)(2,1)}, u32[]{:S(2)}) copy-start(bf16[3,16,512]{2,1,0:T(8,128)(2,1)} %param.15) | copy-start | bytes 147460
  69.3 14.1 %copy-start.3 = (bf16[6,8,64,128]{3,2,1,0:T(8,128)(2,1)S(1)}, bf16[6,8,64,128]{3,2,1,0:T(8,128)(2,1)}, u32[]{:S(2)}) copy-start(bf16[6,8,64,128]{3,2,1,0:T(8,128)(2,1)} %copy-done.2) | copy-start | bytes 2359300
  79.0 0.6 copy-start.8
  79.6 71.7 %all-to-all-start = ((f32[1,3,16,64,128]{4,2,1,0,3:T(8,128)}), f32[1,3,16,64,128]{4,2,1,0,3:T(8,128)S(1)}, u32[]{:S(2)}, u32[]{:S(2)}) async-start(f32[1,3,16,64,128]{4,2,1,0,3:T(8,128)} %copy.202), calls=%async_computation | async-start | bytes 3145728 | tf_op jit(solution)/shard_map/all_to_all | solution.py:72
  83.3 2.7 %copy-start.1 = (s32[512]{0:T(512)S(1)}, s32[512]{0:T(512)}, u32[]{:S(2)}) copy-start(s32[512]{0:T(512)} %param.18) | copy-start | bytes 6148
  83.4 5.0 %copy-start.9 = (f32[16,1,192]{2,1,0:T(1,128)S(1)}, f32[16,1,192]{2,1,0:T(1,128)}, u32[]{:S(2)}) copy-start(f32[16,1,192]{2,1,0:T(1,128)} %copy-done.8) | copy-start | bytes 36868
  89.7 67.9 %copy-start.12 = (f32[64]{0:T(128)S(1)}, f32[64]{0:T(128)}, u32[]{:S(2)}) copy-start(f32[64]{0:T(128)} %param.19) | copy-start | bytes 772
  152.5 7.5 %collective-permute-start = (bf16[3,16,4,128]{3,1,2,0:T(8,128)(2,1)S(1)}, bf16[3,16,4,128]{3,1,2,0:T(8,128)(2,1)S(1)}, u32[]{:S(2)}, u32[]{:S(2)}) collective-permute-start(bf16[3,16,4,128]{3,1,2,0:T(8,128)(2,1)S(1)} %fusion.24), channel_id=1, source_target_pairs={{0,16},{1,17},{2,18},{3,19},{4,20},{5,21},{6,22},{7,23},{8,24},{9,... | collective-permute-start | bytes 147464 | tf_op jit(solution)/shard_map/ppermute | solution.py:12
where the time goes:
time: 165 us; the launch traced here: 162 us
  waiting for transfers between devices  73.3 us (44%)
  starting transfers between devices  35.2 us (21%)
  matrix products  19 us (12%)
  other arithmetic  17.7 us (11%)
  local copies, waits for them, and re-layouts  15.9 us (10%)
    all_to_all x1, waiting for transfers between devices, local(): lax.all_to_all(summed[None], 'seq', split_axis=3, concat_axis=0, tiled=True)  60.5 us
    all_to_all x1, starting transfers between devices, local(): lax.all_to_all(total[None], 'seq', split_axis=3, concat_axis=0, tiled=True)  15.2 us
    all_to_all x1, starting transfers between devices, local(): lax.all_to_all(top[None], 'seq', split_axis=3, concat_axis=0, tiled=True)  11.2 us
    reduce_sum x2, other arithmetic, local(): total = jnp.sum(pre_weights, -1) + jnp.sum(suf_weights, -1)  11.1 us
    all_to_all x1, waiting for transfers between devices, local(): lax.all_to_all(top[None], 'seq', split_axis=3, concat_axis=0, tiled=True)  9.7 us
    dot_general x1, matrix products, local(): jnp.einsum('trkgn,nkd->trkgd', pre_weights.astype(jnp.bfloat16), pre_valu...  8.05 us
    dot_general x1, matrix products, local(): jnp.einsum('trkgd,nkd->trkgn', query, pre_keys, preferred_element_type=jn...  7.9 us
    ppermute x1, starting transfers between devices, shifted(): return lax.ppermute(value, axis, pairs)  5.1 us
  transfers between devices with their start and end apart: 4, of which 4 were waited for; matrix products, arithmetic and copies ran while one was open for 14% of the time, Pallas kernels for 0%

commit v1 on v0

v1 whole, which is shorter than its diff:
```python
import functools

import jax
import jax.numpy as jnp
from jax import lax
from jax.experimental import pallas as pl
from jax.experimental.pallas import tpu as pltpu
from jax.sharding import PartitionSpec as P

HD = 128
LOG2E = 1.4426950408889634
LOW = -1e30
MESH = pl.DeviceIdType.MESH
F32 = jnp.float32
BF16 = jnp.bfloat16


def dot_nt(a, b):
    return lax.dot_general(a, b, (((1,), (1,)), ((), ())), preferred_element_type=F32)


def iota(shape, axis):
    return lax.broadcasted_iota(jnp.int32, shape, axis)


def kernel(
    seq,
    rows_axis,
    q_hbm,
    pk_hbm,
    pv_hbm,
    sk_hbm,
    sv_hbm,
    nk_hbm,
    nv_hbm,
    len_ref,
    pair_ref,
    guide_ref,
    out_ref,
    q_in,
    pk,
    pv,
    sk,
    sv,
    nk,
    nv,
    qb,
    qf,
    o_suf,
    m_suf,
    l_suf,
    send_o,
    send_s,
    recv_o,
    recv_s,
    att_own,
    att_far,
    in_sem,
    send_sem,
    recv_sem,
    att_sem,
):
    steps, row_dev, width = q_in.shape
    heads = width // HD
    kv_heads = pk.shape[1] // HD
    share = heads // seq
    group = heads // kv_heads
    per_kv = seq // kv_heads
    block = share * steps * row_dev
    half = block // 2
    kv_rows = group * steps * row_dev
    combos = group * steps
    suf_dev = sk.shape[1]
    tiles = pk.shape[0] // HD
    hops = seq // 2
    scale = HD**-0.5 * LOG2E

    me = lax.axis_index("seq")
    row = lax.axis_index("row")
    right, left = lax.rem(me + 1, seq), lax.rem(me + seq - 1, seq)
    across = lax.rem(row + rows_axis // 2, rows_axis)
    near = ((right, row), (left, row))

    loads = [
        pltpu.make_async_copy(src, dst, in_sem.at[i])
        for i, (src, dst) in enumerate(
            ((q_hbm, q_in), (sk_hbm, sk), (sv_hbm, sv), (pk_hbm, pk), (pv_hbm, pv), (nk_hbm, nk), (nv_hbm, nv))
        )
    ]
    for load in loads:
        load.start()

    barrier = pltpu.get_barrier_semaphore()
    for device in (*near, (me, across)):
        pl.semaphore_signal(barrier, inc=1, device_id=device, device_id_type=MESH)
    pl.semaphore_wait(barrier, 3)

    loads[0].wait()
    for head in range(heads):
        for t in range(steps):
            tile = q_in[t, :, head * HD : (head + 1) * HD]
            at = (head * steps + t) * row_dev
            qb[at : at + row_dev, :] = tile
            qf[at : at + row_dev, :] = tile.astype(F32)

    loads[1].wait()
    loads[2].wait()
    zeros = jnp.zeros((suf_dev, HD), BF16)
    ones = jnp.ones((suf_dev, HD), BF16)
    first_half = iota((combos, 2 * suf_dev), 1) < suf_dev
    spot = me * suf_dev + lax.rem(iota((combos, 2 * suf_dev), 1), suf_dev)

    def beside(a, b):
        top = jnp.concatenate([a, zeros], 1)
        low = jnp.concatenate([zeros, b], 1)
        return jnp.concatenate([top, low], 0)

    def suffix_row(r):
        live = spot < len_ref[r]
        for pair in range(kv_heads // 2):
            g0, g1 = 2 * pair, 2 * pair + 1
            at0 = pl.ds(g0 * kv_rows + r, combos, stride=row_dev)
            at1 = pl.ds(g1 * kv_rows + r, combos, stride=row_dev)
            q2 = jnp.concatenate([qf[at0, :], qf[at1, :]], 1).astype(BF16)
            k0 = sk[r, :, g0 * HD : (g0 + 1) * HD]
            k1 = sk[r, :, g1 * HD : (g1 + 1) * HD]
            s = dot_nt(q2, beside(k0, k1)) * scale
            s = jnp.where(live, s, LOW)
            m0 = jnp.max(jnp.where(first_half, s, LOW), 1, keepdims=True)
            m1 = jnp.max(jnp.where(first_half, LOW, s), 1, keepdims=True)
            w = jnp.exp2(s - jnp.where(first_half, m0, m1)).astype(BF16)
            v0 = sv[r, :, g0 * HD : (g0 + 1) * HD]
            v1 = sv[r, :, g1 * HD : (g1 + 1) * HD]
            values = jnp.concatenate([beside(v0, v1), beside(ones, ones)], 1)
            o = jnp.dot(w, values, preferred_element_type=F32)
            o_suf[at0, :] = o[:, :HD]
            o_suf[at1, :] = o[:, HD : 2 * HD]
            l_suf[at0, :] = o[:, 2 * HD : 3 * HD]
            l_suf[at1, :] = o[:, 3 * HD :]
            m_suf[at0, :] = jnp.broadcast_to(m0, (combos, HD))
            m_suf[at1, :] = jnp.broadcast_to(m1, (combos, HD))

    def suffix_rows(i, carry):
        for j in range(4):
            suffix_row(i * 4 + j)
        return carry

    lax.fori_loop(0, row_dev // 4, suffix_rows, 0)

    loads[3].wait()
    loads[4].wait()
    loads[5].wait()
    loads[6].wait()
    many_ones = jnp.ones((pk.shape[0], HD), BF16)

    def partial(dest):
        at = pl.ds(pl.multiple_of(dest * block, block), block)
        lanes = pl.ds(pl.multiple_of((dest // per_kv) * HD, HD), HD)
        s = dot_nt(qb[at, :], pk[:, lanes])
        m_low = m_suf[at, :]
        m = jnp.maximum(jnp.max(s, 1, keepdims=True) * scale, m_low)
        w = jnp.concatenate(
            [jnp.exp2(s[:, j * HD : (j + 1) * HD] * scale - m).astype(BF16) for j in range(tiles)], 1
        )
        values = jnp.concatenate([pv[:, lanes], many_ones], 1)
        o = jnp.dot(w, values, preferred_element_type=F32)
        f = jnp.exp2(m_low - m)
        total = o[:, HD:] + f * l_suf[at, :]
        return (o[:, :HD] + f * o_suf[at, :]) / total, m + jnp.log2(total)

    diagonal = iota((half, HD), 0) == iota((half, HD), 1)

    def flat(lse):
        return jnp.broadcast_to(jnp.sum(jnp.where(diagonal, lse, 0.0), 0, keepdims=True), (8, HD))

    def merge(o, stat, arrived_o, arrived_stat):
        gap = stat - arrived_stat
        weight = 1.0 / (1.0 + jnp.exp2(gap))
        column = jnp.sum(
            jnp.where(diagonal, jnp.broadcast_to(weight[:1], (half, HD)), 0.0), 1, keepdims=True
        )
        merged = o + column * (arrived_o.astype(F32) - o)
        return merged, jnp.maximum(stat, arrived_stat) + jnp.log2(1.0 + jnp.exp2(-jnp.abs(gap)))

    def copies(way, k, first, size):
        stat_at = pl.ds(first // half * 8, size // half * 8)
        return (
            pltpu.make_async_remote_copy(
                src_ref=send_o.at[way, k, pl.ds(first, size)],
                dst_ref=recv_o.at[way, k, pl.ds(first, size)],
                send_sem=send_sem.at[way, k, 0],
                recv_sem=recv_sem.at[way, k, 0],
                device_id=near[way],
                device_id_type=MESH,
            ),
            pltpu.make_async_remote_copy(
                src_ref=send_s.at[way, k, stat_at],
                dst_ref=recv_s.at[way, k, stat_at],
                send_sem=send_sem.at[way, k, 1],
                recv_sem=recv_sem.at[way, k, 1],
                device_id=near[way],
                device_id_type=MESH,
            ),
        )

    o, lse = partial(lax.rem(me + hops, seq))
    for way in range(2):
        part = slice(way * half, (way + 1) * half)
        send_o[way, 0, part, :] = o[part].astype(BF16)
        send_s[way, 0, way * 8 : way * 8 + 8, :] = flat(lse[part])
        for copy in copies(way, 0, way * half, half):
            copy.start()

    def hop(k, only):
        for way in range(2):
            dest = lax.rem(me + hops - k, seq) if way == 0 else lax.rem(me + seq - hops + k, seq)
            o, lse = partial(dest)
            stats = [flat(lse[:half]), flat(lse[half:])]
            if only:
                for copy in copies(way, 0, way * half, half):
                    copy.wait_recv()
            else:
                for copy in copies(way, k - 1, 0, block):
                    copy.wait_recv()
            for piece in range(2):
                part = slice(piece * half, (piece + 1) * half)
                stat_part = slice(piece * 8, piece * 8 + 8)
                o_piece, stat = o[part], stats[piece]
                if not only or piece == way:
                    o_piece, stat = merge(
                        o_piece, stat, recv_o[way, k - 1, part, :], recv_s[way, k - 1, stat_part, :]
                    )
                send_o[way, k, part, :] = o_piece.astype(BF16)
                send_s[way, k, stat_part, :] = stat
            for copy in copies(way, k, 0, block):
                copy.start()

    hop(1, True)

    def one_hop(k, carry):
        hop(k, False)
        return carry

    lax.fori_loop(2, hops, one_hop, 0)

    o, lse = partial(me)
    own_at = pl.multiple_of(me * block, block)
    lanes = pl.ds(pl.multiple_of((me // per_kv) * HD, HD), HD)
    new_k = [nk[j, :, lanes].astype(F32) for j in range(steps)]
    new_v = [nv[j, :, lanes].astype(F32) for j in range(steps)]
    own_o, own_lse = [], []
    for head in range(share):
        for t in range(steps):
            i = (head * steps + t) * row_dev
            query = qf[pl.ds(own_at + i, row_dev), :]
            fresh = [jnp.sum(query * new_k[j], 1, keepdims=True) * scale for j in range(t + 1)]
            base = lse[i : i + row_dev]
            top = base
            for score in fresh:
                top = jnp.maximum(top, score)
            weight = jnp.exp2(base - top)
            total, summed = weight, weight * o[i : i + row_dev]
            for j in range(t + 1):
                weight = jnp.exp2(fresh[j] - top)
                total = total + weight
                summed = summed + weight * new_v[j]
            own_o.append(summed / total)
            own_lse.append(top + jnp.log2(total))
    o = jnp.concatenate(own_o, 0)
    lse = jnp.concatenate(own_lse, 0)
    own = [(o[:half], flat(lse[:half])), (o[half:], flat(lse[half:]))]
    for way in range(2):
        for copy in copies(way, hops - 1, 0, block):
            copy.wait_recv()
        own = [
            merge(
                *own[piece],
                recv_o[way, hops - 1, piece * half : (piece + 1) * half, :],
                recv_s[way, hops - 1, piece * 8 : piece * 8 + 8, :],
            )
            for piece in range(2)
        ]
    for piece in range(2):
        att_own[piece * half : (piece + 1) * half, :] = own[piece][0].astype(BF16)

    swap = pltpu.make_async_remote_copy(
        src_ref=att_own,
        dst_ref=att_far,
        send_sem=att_sem.at[0],
        recv_sem=att_sem.at[1],
        device_id=(me, across),
        device_id_type=MESH,
    )
    swap.start()
    place = jnp.zeros((row_dev, row_dev), jnp.int32)
    for r in range(row_dev):
        partner = lax.rem(pair_ref[row * row_dev + r], row_dev)
        place = jnp.where(iota((row_dev, row_dev), 0) == r, partner, place)
    chosen = jnp.where(place == iota((row_dev, row_dev), 1), 1.0, 0.0).astype(BF16)
    is_low = jnp.broadcast_to(row, (row_dev, HD)) < rows_axis // 2
    swap.wait_recv()
    for head in range(share):
        guide = guide_ref[me * share + head]
        for t in range(steps):
            i = (head * steps + t) * row_dev
            mine = att_own[i : i + row_dev, :].astype(F32)
            other = jnp.dot(chosen, att_far[i : i + row_dev, :], preferred_element_type=F32)
            cond = jnp.where(is_low, mine, other)
            uncond = jnp.where(is_low, other, mine)
            mix = uncond + guide * (cond - uncond)
            norm = jnp.sqrt(jnp.mean(mix * mix, 1, keepdims=True) + 1e-06)
            out_ref[t, :, head * HD : (head + 1) * HD] = (mix / norm).astype(BF16)

    swap.wait_send()
    for way in range(2):
        for copy in copies(way, 0, way * half, half):
            copy.wait_send()

    def drain(k, carry):
        for way in range(2):
            for copy in copies(way, k, 0, block):
                copy.wait_send()
        return carry

    lax.fori_loop(1, hops, drain, 0)


def local(seq, rows_axis, queries, pk, pv, sk, sv, nk, nv, lengths, pair_of, guidance):
    steps, row_dev, width = queries.shape
    heads = width // HD
    share = heads // seq
    block = share * steps * row_dev
    hops = seq // 2
    whole = heads * steps * row_dev
    hbm = pl.BlockSpec(memory_space=pl.ANY)
    smem = pl.BlockSpec(memory_space=pltpu.SMEM)
    return pl.pallas_call(
        functools.partial(kernel, seq, rows_axis),
        out_shape=jax.ShapeDtypeStruct((steps, row_dev, share * HD), BF16),
        in_specs=[hbm] * 7 + [smem] * 3,
        out_specs=pl.BlockSpec(memory_space=pltpu.VMEM),
        scratch_shapes=[
            *(pltpu.VMEM(a.shape, a.dtype) for a in (queries, pk, pv, sk, sv, nk, nv)),
            pltpu.VMEM((whole, HD), BF16),
            pltpu.VMEM((whole, HD), F32),
            pltpu.VMEM((whole, HD), F32),
            pltpu.VMEM((whole, HD), F32),
            pltpu.VMEM((whole, HD), F32),
            pltpu.VMEM((2, hops, block, HD), BF16),
            pltpu.VMEM((2, hops, 16, HD), F32),
            pltpu.VMEM((2, hops, block, HD), BF16),
            pltpu.VMEM((2, hops, 16, HD), F32),
            pltpu.VMEM((block, HD), BF16),
            pltpu.VMEM((block, HD), BF16),
            pltpu.SemaphoreType.DMA((7,)),
            pltpu.SemaphoreType.DMA((2, hops, 2)),
            pltpu.SemaphoreType.DMA((2, hops, 2)),
            pltpu.SemaphoreType.DMA((2,)),
        ],
        compiler_params=pltpu.CompilerParams(
            collective_id=0, has_side_effects=True, vmem_limit_bytes=56 * 1024 * 1024
        ),
    )(queries, pk, pv, sk, sv, nk, nv, lengths, pair_of, guidance)


def solution(mesh):
    placed = (
        P(None, "row", None),
        P("seq", None),
        P("seq", None),
        P("row", "seq", None),
        P("row", "seq", None),
        P(None, "row", None),
        P(None, "row", None),
        P("row"),
        P(),
        P(),
    )
    body = functools.partial(local, mesh.shape["seq"], mesh.shape["row"])
    return jax.shard_map(
        body, mesh=mesh, in_specs=placed, out_specs=P(None, "row", "seq"), check_vma=False
    )
```

time: 165 us -> 53.7 us (0.33); the launches traced: 162 us -> 52.8 us
  waiting for transfers between devices: 73.3 us -> 0 us
  Pallas kernels: 0 us -> 51.4 us
  starting transfers between devices: 35.2 us -> 0 us
  matrix products: 19 us -> 0 us
  other arithmetic: 17.7 us -> 0 us
  local copies, waits for them, and re-layouts: 15.9 us -> 1.42 us
    all_to_all x3 -> x0, waiting for transfers between devices: 71 us -> none  [the longest x1 60.5 us: local(): lax.all_to_all(summed[None], 'seq', split_axis=3, concat_axis=0, tiled=True)]
    pallas_call x0 -> x1, Pallas kernels: none -> 51.4 us  [local(): pl.pallas_call(functools.partial(kernel, seq, rows_axis), out_shape=jax.S...]
    all_to_all x3 -> x0, starting transfers between devices: 30.1 us -> none  [the longest x1 15.2 us: local(): lax.all_to_all(total[None], 'seq', split_axis=3, concat_axis=0, tiled=True)]
    dot_general x6 -> x0, matrix products: 19 us -> none  [the longest x1 8.05 us: local(): jnp.einsum('trkgn,nkd->trkgd', pre_weights.astype(jnp.bfloat16), pre_valu...]
    reduce_sum x6 -> x0, other arithmetic: 12.5 us -> none  [the longest x2 11.1 us: local(): total = jnp.sum(pre_weights, -1) + jnp.sum(suf_weights, -1)]
    reshape x7 -> x0, local copies, waits for them, and re-layouts: 5.5 us -> none  [the longest x1 2.37 us: local(): pre_keys = prefix_keys.reshape(-1, kv_heads, HD)]
    ppermute x1 -> x0, starting transfers between devices: 5.1 us -> none  [shifted(): return lax.ppermute(value, axis, pairs)]
    unnamed x32 -> x1, local copies, waits for them, and re-layouts: 4.47 us -> 1.42 us
  transfers between devices with their start and end apart: 4 -> 0, of which waited for: 4 -> 0; matrix products, arithmetic and copies ran while one was open for 14% -> 0% of each run, Pallas kernels for 0% -> 0%
where the time goes in v1:
time: 53.7 us; the launch traced here: 52.8 us
  Pallas kernels  51.4 us (96%)
  local copies, waits for them, and re-layouts  1.42 us (3%)
    pallas_call x1, Pallas kernels, local(): pl.pallas_call(functools.partial(kernel, seq, rows_axis), out_shape=jax.S...  51.4 us
    unnamed x1, local copies, waits for them, and re-layouts  1.42 us

profile of v1, /device:TPU:6, one launch (start us, length us, event | category | flops | bytes accessed | tf_op | source)
XLA Modules:
  0.0 52.8 jit_solution(5123668390307922249)
XLA Ops:
  0.0 51.4 %shard_map.100 = bf16[3,16,512]{2,1,0:T(8,128)(2,1)} custom-call(bf16[3,16,8192]{2,1,0:T(8,128)(2,1)} %q_hbm.1, bf16[1536,512]{1,0:T(8,128)(2,1)} %pk_hbm.1, bf16[1536,512]{1,0:T(8,128)(2,1)} %pv_hbm.1, bf16[16,64,512]{2,1,0:T(8,128)(2,1)} %sk_hbm.1, bf16[16,64,512]{2,1,0:T(8,128)(2,1)} %sv_hbm.1, bf16[3,16,512]{2,1,0:T(8,128)(2,1)} %nk_hbm.1, ...), custom_call_target="tpu_custom_call" | custom-call | tf_op jit(solution)/shard_map/pallas_call | solution.py:337
  51.4 1.4 %copy.12 = bf16[3,16,512]{2,1,0:T(8,128)(2,1)} copy(bf16[3,16,512]{2,1,0:T(8,128)(2,1)} %shard_map.100) | data formatting | bytes 98304

commit v2 on v1

--- a/solution.py
+++ b/solution.py
@@ -11,6 +11,9 @@
 LOG2E = 1.4426950408889634
 LOW = -1e30
 MESH = pl.DeviceIdType.MESH
+PARENT = {1: 0, 2: 0, 3: 2, 4: 2, 5: 4, 6: 4, 7: 6, 8: 6}
+ORDER = (7, 6, 5, 4, 3, 2, 1)
+MERGES = {4: (6,), 2: (4,), 1: (2,)}
 F32 = jnp.float32
 BF16 = jnp.bfloat16
 
@@ -49,15 +52,18 @@
     o_suf,
     m_suf,
     l_suf,
-    send_o,
-    send_s,
-    recv_o,
-    recv_s,
-    att_own,
-    att_far,
+    send,
+    recv,
+    own_o,
+    own_s,
+    recv_far,
+    own_msg,
+    far_msg,
     in_sem,
     send_sem,
     recv_sem,
+    send_far_sem,
+    recv_far_sem,
     att_sem,
 ):
     steps, row_dev, width = q_in.shape
@@ -77,9 +83,13 @@
 
     me = lax.axis_index("seq")
     row = lax.axis_index("row")
-    right, left = lax.rem(me + 1, seq), lax.rem(me + seq - 1, seq)
     across = lax.rem(row + rows_axis // 2, rows_axis)
-    near = ((right, row), (left, row))
+    spans = sorted({d - p for d, p in PARENT.items()})
+
+    last = [d for d in PARENT if PARENT[d] == 0]
+
+    def reach(way, span, column):
+        return (lax.rem(me + (span if way == 0 else seq - span), seq), column)
 
     loads = [
         pltpu.make_async_copy(src, dst, in_sem.at[i])
@@ -91,9 +101,10 @@
         load.start()
 
     barrier = pltpu.get_barrier_semaphore()
-    for device in (*near, (me, across)):
+    peers = [reach(way, span, row) for span in spans for way in range(2)]
+    peers += [reach(way, span, across) for span in last for way in range(2)] + [(me, across)]
+    for device in peers:
         pl.semaphore_signal(barrier, inc=1, device_id=device, device_id_type=MESH)
-    pl.semaphore_wait(barrier, 3)
 
     loads[0].wait()
     for head in range(heads):
@@ -141,11 +152,11 @@
             m_suf[at1, :] = jnp.broadcast_to(m1, (combos, HD))
 
     def suffix_rows(i, carry):
-        for j in range(4):
-            suffix_row(i * 4 + j)
+        for j in range(8):
+            suffix_row(i * 8 + j)
         return carry
 
-    lax.fori_loop(0, row_dev // 4, suffix_rows, 0)
+    lax.fori_loop(0, row_dev // 8, suffix_rows, 0)
 
     loads[3].wait()
     loads[4].wait()
@@ -153,10 +164,13 @@
     loads[6].wait()
     many_ones = jnp.ones((pk.shape[0], HD), BF16)
 
-    def partial(dest):
+    def scores(dest):
+        at = pl.ds(pl.multiple_of(dest * block, block), block)
+        return dot_nt(qb[at, :], pk[:, pl.ds(pl.multiple_of((dest // per_kv) * HD, HD), HD)])
+
+    def attend(dest, s):
         at = pl.ds(pl.multiple_of(dest * block, block), block)
         lanes = pl.ds(pl.multiple_of((dest // per_kv) * HD, HD), HD)
-        s = dot_nt(qb[at, :], pk[:, lanes])
         m_low = m_suf[at, :]
         m = jnp.maximum(jnp.max(s, 1, keepdims=True) * scale, m_low)
         w = jnp.concatenate(
@@ -168,10 +182,33 @@
         total = o[:, HD:] + f * l_suf[at, :]
         return (o[:, :HD] + f * o_suf[at, :]) / total, m + jnp.log2(total)
 
+    def partial(dest):
+        return attend(dest, scores(dest))
+
+    def partials(dests):
+        s = [scores(dest) for dest in dests]
+        return [attend(dest, one) for dest, one in zip(dests, s)]
+
     diagonal = iota((half, HD), 0) == iota((half, HD), 1)
 
     def flat(lse):
         return jnp.broadcast_to(jnp.sum(jnp.where(diagonal, lse, 0.0), 0, keepdims=True), (8, HD))
+
+    row_in_tile = iota((8, HD), 0)
+
+    def packed(stats):
+        tiles = []
+        for stat in stats:
+            high = stat.astype(BF16).astype(F32)
+            middle = (stat - high).astype(BF16).astype(F32)
+            low = stat - high - middle
+            tile = jnp.where(row_in_tile == 0, high, jnp.where(row_in_tile == 1, middle, low))
+            tiles.append(jnp.where(row_in_tile < 3, tile, 0.0))
+        return jnp.concatenate(tiles, 0).astype(BF16)
+
+    def unpacked(rows, piece):
+        tile = rows.astype(F32)[piece * 8 : piece * 8 + 8]
+        return jnp.broadcast_to(jnp.sum(tile, 0, keepdims=True), (8, HD))
 
     def merge(o, stat, arrived_o, arrived_stat):
         gap = stat - arrived_stat
@@ -182,66 +219,99 @@
         merged = o + column * (arrived_o.astype(F32) - o)
         return merged, jnp.maximum(stat, arrived_stat) + jnp.log2(1.0 + jnp.exp2(-jnp.abs(gap)))
 
-    def copies(way, k, first, size):
-        stat_at = pl.ds(first // half * 8, size // half * 8)
-        return (
-            pltpu.make_async_remote_copy(
-                src_ref=send_o.at[way, k, pl.ds(first, size)],
-                dst_ref=recv_o.at[way, k, pl.ds(first, size)],
-                send_sem=send_sem.at[way, k, 0],
-                recv_sem=recv_sem.at[way, k, 0],
-                device_id=near[way],
-                device_id_type=MESH,
-            ),
-            pltpu.make_async_remote_copy(
-                src_ref=send_s.at[way, k, stat_at],
-                dst_ref=recv_s.at[way, k, stat_at],
-                send_sem=send_sem.at[way, k, 1],
-                recv_sem=recv_sem.at[way, k, 1],
-                device_id=near[way],
-                device_id_type=MESH,
-            ),
+    def message(way, d):
+        size = 16 + (half if d == hops else block)
+        return pltpu.make_async_remote_copy(
+            src_ref=send.at[way, d - 1, pl.ds(0, size)],
+            dst_ref=recv.at[way, d - 1, pl.ds(0, size)],
+            send_sem=send_sem.at[way, d - 1],
+            recv_sem=recv_sem.at[way, d - 1],
+            device_id=reach(way, d - PARENT[d], row),
+            device_id_type=MESH,
         )
 
+    def message_across(way, d):
+        return pltpu.make_async_remote_copy(
+            src_ref=send.at[way, d - 1],
+            dst_ref=recv_far.at[way, d - 1],
+            send_sem=send_far_sem.at[way, d - 1],
+            recv_sem=recv_far_sem.at[way, d - 1],
+            device_id=reach(way, d, across),
+            device_id_type=MESH,
+        )
+
+    def send_on(way, d):
+        message(way, d).start()
+        if PARENT[d] == 0:
+            message_across(way, d).start()
+
     o, lse = partial(lax.rem(me + hops, seq))
+    stats = packed([flat(lse[:half]), flat(lse[half:])])
+    pl.semaphore_wait(barrier, len(peers))
     for way in range(2):
-        part = slice(way * half, (way + 1) * half)
-        send_o[way, 0, part, :] = o[part].astype(BF16)
-        send_s[way, 0, way * 8 : way * 8 + 8, :] = flat(lse[part])
-        for copy in copies(way, 0, way * half, half):
-            copy.start()
-
-    def hop(k, only):
+        send[way, hops - 1, :16, :] = stats
+        send[way, hops - 1, 16 : 16 + half, :] = o[way * half : (way + 1) * half].astype(BF16)
+        message(way, hops).start()
+
+    children = {p: [d for d in PARENT if PARENT[d] == p] for p in range(hops)}
+
+    def gather(way, d, pieces):
+        for child in sorted(children[d]):
+            message(way, child).wait_recv()
+            stats = recv[way, child - 1, :16, :]
+            for piece in range(2):
+                if child == hops and piece != way:
+                    continue
+                at = 16 if child == hops else 16 + piece * half
+                pieces[piece] = merge(
+                    *pieces[piece], recv[way, child - 1, at : at + half, :], unpacked(stats, piece)
+                )
+        return pieces
+
+    def pass_on(d):
         for way in range(2):
-            dest = lax.rem(me + hops - k, seq) if way == 0 else lax.rem(me + seq - hops + k, seq)
-            o, lse = partial(dest)
+            pieces = [
+                (
+                    own_o[way, d - 1, piece * half : (piece + 1) * half, :],
+                    own_s[way, d - 1, piece * 8 : piece * 8 + 8, :],
+                )
+                for piece in range(2)
+            ]
+            pieces = gather(way, d, pieces)
+            send[way, d - 1, :16, :] = packed([stat for _, stat in pieces])
+            for piece in range(2):
+                at = 16 + piece * half
+                send[way, d - 1, at : at + half, :] = pieces[piece][0].astype(BF16)
+            send_on(way, d)
+
+    def step(k, carry):
+        d = jnp.int32(ORDER[0])
+        for i in range(1, len(ORDER)):
+            d = jnp.where(k == i, ORDER[i], d)
+        dests = [lax.rem(me + (d if way == 0 else seq - d), seq) for way in range(2)]
+        found = partials(dests)
+        for way in range(2):
+            o, lse = found[way]
             stats = [flat(lse[:half]), flat(lse[half:])]
-            if only:
-                for copy in copies(way, 0, way * half, half):
-                    copy.wait_recv()
-            else:
-                for copy in copies(way, k - 1, 0, block):
-                    copy.wait_recv()
-            for piece in range(2):
-                part = slice(piece * half, (piece + 1) * half)
-                stat_part = slice(piece * 8, piece * 8 + 8)
-                o_piece, stat = o[part], stats[piece]
-                if not only or piece == way:
-                    o_piece, stat = merge(
-                        o_piece, stat, recv_o[way, k - 1, part, :], recv_s[way, k - 1, stat_part, :]
-                    )
-                send_o[way, k, part, :] = o_piece.astype(BF16)
-                send_s[way, k, stat_part, :] = stat
-            for copy in copies(way, k, 0, block):
-                copy.start()
-
-    hop(1, True)
-
-    def one_hop(k, carry):
-        hop(k, False)
+            send[way, d - 1, :16, :] = packed(stats)
+            send[way, d - 1, 16:, :] = o.astype(BF16)
+            own_o[way, d - 1] = o
+            own_s[way, d - 1] = jnp.concatenate(stats, 0)
+        for way in range(2):
+            for i in range(len(ORDER)):
+                if not children[ORDER[i]]:
+                    pl.when(k == i)(lambda way=way, i=i: send_on(way, ORDER[i]))
+        for i in range(len(ORDER)):
+            if MERGES.get(ORDER[i]):
+
+                def merges(i=i):
+                    for at in MERGES[ORDER[i]]:
+                        pass_on(at)
+
+                pl.when(k == i)(merges)
         return carry
 
-    lax.fori_loop(2, hops, one_hop, 0)
+    lax.fori_loop(0, len(ORDER), step, 0)
 
     o, lse = partial(me)
     own_at = pl.multiple_of(me * block, block)
@@ -269,23 +339,11 @@
     o = jnp.concatenate(own_o, 0)
     lse = jnp.concatenate(own_lse, 0)
     own = [(o[:half], flat(lse[:half])), (o[half:], flat(lse[half:]))]
-    for way in range(2):
-        for copy in copies(way, hops - 1, 0, block):
-            copy.wait_recv()
-        own = [
-            merge(
-                *own[piece],
-                recv_o[way, hops - 1, piece * half : (piece + 1) * half, :],
-                recv_s[way, hops - 1, piece * 8 : piece * 8 + 8, :],
-            )
-            for piece in range(2)
-        ]
-    for piece in range(2):
-        att_own[piece * half : (piece + 1) * half, :] = own[piece][0].astype(BF16)
-
+    own_msg[:16, :] = packed([stat for _, stat in own])
+    own_msg[16:, :] = o.astype(BF16)
     swap = pltpu.make_async_remote_copy(
-        src_ref=att_own,
-        dst_ref=att_far,
+        src_ref=own_msg,
+        dst_ref=far_msg,
         send_sem=att_sem.at[0],
         recv_sem=att_sem.at[1],
         device_id=(me, across),
@@ -298,13 +356,46 @@
         place = jnp.where(iota((row_dev, row_dev), 0) == r, partner, place)
     chosen = jnp.where(place == iota((row_dev, row_dev), 1), 1.0, 0.0).astype(BF16)
     is_low = jnp.broadcast_to(row, (row_dev, HD)) < rows_axis // 2
+
+    def take(pieces, buffer, way, child):
+        stats = buffer[way, child - 1, :16, :]
+        return [
+            merge(
+                *pieces[piece],
+                buffer[way, child - 1, 16 + piece * half : 16 + (piece + 1) * half, :],
+                unpacked(stats, piece),
+            )
+            for piece in range(2)
+        ]
+
+    for child in last[:-1]:
+        for way in range(2):
+            message(way, child).wait_recv()
+            own = take(own, recv, way, child)
     swap.wait_recv()
+    stats = far_msg[:16, :]
+    far = [
+        (far_msg[16 + piece * half : 16 + (piece + 1) * half, :].astype(F32), unpacked(stats, piece))
+        for piece in range(2)
+    ]
+    for child in last[:-1]:
+        for way in range(2):
+            message_across(way, child).wait_recv()
+            far = take(far, recv_far, way, child)
+    for way in range(2):
+        message(way, last[-1]).wait_recv()
+        own = take(own, recv, way, last[-1])
+    for way in range(2):
+        message_across(way, last[-1]).wait_recv()
+        far = take(far, recv_far, way, last[-1])
+    o = jnp.concatenate([own[0][0], own[1][0]], 0).astype(BF16)
+    o_far = jnp.concatenate([far[0][0], far[1][0]], 0).astype(BF16)
     for head in range(share):
         guide = guide_ref[me * share + head]
         for t in range(steps):
             i = (head * steps + t) * row_dev
-            mine = att_own[i : i + row_dev, :].astype(F32)
-            other = jnp.dot(chosen, att_far[i : i + row_dev, :], preferred_element_type=F32)
+            mine = o[i : i + row_dev].astype(F32)
+            other = jnp.dot(chosen, o_far[i : i + row_dev], preferred_element_type=F32)
             cond = jnp.where(is_low, mine, other)
             uncond = jnp.where(is_low, other, mine)
             mix = uncond + guide * (cond - uncond)
@@ -313,16 +404,10 @@
 
     swap.wait_send()
     for way in range(2):
-        for copy in copies(way, 0, way * half, half):
-            copy.wait_send()
-
-    def drain(k, carry):
-        for way in range(2):
-            for copy in copies(way, k, 0, block):
-                copy.wait_send()
-        return carry
-
-    lax.fori_loop(1, hops, drain, 0)
+        for d in PARENT:
+            message(way, d).wait_send()
+        for d in last:
+            message_across(way, d).wait_send()
 
 
 def local(seq, rows_axis, queries, pk, pv, sk, sv, nk, nv, lengths, pair_of, guidance):
@@ -346,15 +431,18 @@
             pltpu.VMEM((whole, HD), F32),
             pltpu.VMEM((whole, HD), F32),
             pltpu.VMEM((whole, HD), F32),
-            pltpu.VMEM((2, hops, block, HD), BF16),
-            pltpu.VMEM((2, hops, 16, HD), F32),
-            pltpu.VMEM((2, hops, block, HD), BF16),
-            pltpu.VMEM((2, hops, 16, HD), F32),
-            pltpu.VMEM((block, HD), BF16),
-            pltpu.VMEM((block, HD), BF16),
+            pltpu.VMEM((2, hops, 16 + block, HD), BF16),
+            pltpu.VMEM((2, hops, 16 + block, HD), BF16),
+            pltpu.VMEM((2, hops - 1, block, HD), F32),
+            pltpu.VMEM((2, hops - 1, 16, HD), F32),
+            pltpu.VMEM((2, max(d for d in PARENT if PARENT[d] == 0), 16 + block, HD), BF16),
+            pltpu.VMEM((16 + block, HD), BF16),
+            pltpu.VMEM((16 + block, HD), BF16),
             pltpu.SemaphoreType.DMA((7,)),
-            pltpu.SemaphoreType.DMA((2, hops, 2)),
-            pltpu.SemaphoreType.DMA((2, hops, 2)),
+            pltpu.SemaphoreType.DMA((2, hops)),
+            pltpu.SemaphoreType.DMA((2, hops)),
+            pltpu.SemaphoreType.DMA((2, hops)),
+            pltpu.SemaphoreType.DMA((2, hops)),
             pltpu.SemaphoreType.DMA((2,)),
         ],
         compiler_params=pltpu.CompilerParams(

time: 53.7 us -> 42.5 us (0.79); the launches traced: 52.8 us -> 42.2 us
  Pallas kernels: 51.4 us -> 40.8 us
    pallas_call x1, Pallas kernels: 51.4 us -> 40.8 us  [local(): pl.pallas_call(functools.partial(kernel, seq, rows_axis), out_shape=jax.S...]
where the time goes in v2:
time: 42.5 us; the launch traced here: 42.2 us
  Pallas kernels  40.8 us (96%)
  local copies, waits for them, and re-layouts  1.42 us (3%)
    pallas_call x1, Pallas kernels, local(): pl.pallas_call(functools.partial(kernel, seq, rows_axis), out_shape=jax.S...  40.8 us
    unnamed x1, local copies, waits for them, and re-layouts  1.42 us

profile of v2, /device:TPU:6, one launch (start us, length us, event | category | flops | bytes accessed | tf_op | source)
XLA Modules:
  0.0 42.2 jit_solution(18143668286716973921)
XLA Ops:
  0.0 40.8 %shard_map.100 = bf16[3,16,512]{2,1,0:T(8,128)(2,1)} custom-call(bf16[3,16,8192]{2,1,0:T(8,128)(2,1)} %q_hbm.1, bf16[1536,512]{1,0:T(8,128)(2,1)} %pk_hbm.1, bf16[1536,512]{1,0:T(8,128)(2,1)} %pv_hbm.1, bf16[16,64,512]{2,1,0:T(8,128)(2,1)} %sk_hbm.1, bf16[16,64,512]{2,1,0:T(8,128)(2,1)} %sv_hbm.1, bf16[3,16,512]{2,1,0:T(8,128)(2,1)} %nk_hbm.1, ...), custom_call_target="tpu_custom_call" | custom-call | tf_op jit(solution)/shard_map/pallas_call | solution.py:422
  40.8 1.4 %copy.12 = bf16[3,16,512]{2,1,0:T(8,128)(2,1)} copy(bf16[3,16,512]{2,1,0:T(8,128)(2,1)} %shard_map.100) | data formatting | bytes 98304

commit v3 on v2

--- a/solution.py
+++ b/solution.py
@@ -13,7 +13,8 @@
 MESH = pl.DeviceIdType.MESH
 PARENT = {1: 0, 2: 0, 3: 2, 4: 2, 5: 4, 6: 4, 7: 6, 8: 6}
 ORDER = (7, 6, 5, 4, 3, 2, 1)
-MERGES = {4: (6,), 2: (4,), 1: (2,)}
+EARLY = 4
+MERGES = {5: (6,), 3: (4,), 1: (2,)}
 F32 = jnp.float32
 BF16 = jnp.bfloat16
 
@@ -59,6 +60,8 @@
     recv_far,
     own_msg,
     far_msg,
+    att_own,
+    att_far,
     in_sem,
     send_sem,
     recv_sem,
@@ -151,12 +154,8 @@
             m_suf[at0, :] = jnp.broadcast_to(m0, (combos, HD))
             m_suf[at1, :] = jnp.broadcast_to(m1, (combos, HD))
 
-    def suffix_rows(i, carry):
-        for j in range(8):
-            suffix_row(i * 8 + j)
-        return carry
-
-    lax.fori_loop(0, row_dev // 8, suffix_rows, 0)
+    for r in range(row_dev):
+        suffix_row(r)
 
     loads[3].wait()
     loads[4].wait()
@@ -240,10 +239,13 @@
             device_id_type=MESH,
         )
 
+    def early(way, d):
+        return lax.rem(me + (d if way == 0 else seq - d), seq) < EARLY
+
     def send_on(way, d):
         message(way, d).start()
         if PARENT[d] == 0:
-            message_across(way, d).start()
+            pl.when(early(way, d))(lambda: message_across(way, d).start())
 
     o, lse = partial(lax.rem(me + hops, seq))
     stats = packed([flat(lse[:half]), flat(lse[half:])])
@@ -339,24 +341,6 @@
     o = jnp.concatenate(own_o, 0)
     lse = jnp.concatenate(own_lse, 0)
     own = [(o[:half], flat(lse[:half])), (o[half:], flat(lse[half:]))]
-    own_msg[:16, :] = packed([stat for _, stat in own])
-    own_msg[16:, :] = o.astype(BF16)
-    swap = pltpu.make_async_remote_copy(
-        src_ref=own_msg,
-        dst_ref=far_msg,
-        send_sem=att_sem.at[0],
-        recv_sem=att_sem.at[1],
-        device_id=(me, across),
-        device_id_type=MESH,
-    )
-    swap.start()
-    place = jnp.zeros((row_dev, row_dev), jnp.int32)
-    for r in range(row_dev):
-        partner = lax.rem(pair_ref[row * row_dev + r], row_dev)
-        place = jnp.where(iota((row_dev, row_dev), 0) == r, partner, place)
-    chosen = jnp.where(place == iota((row_dev, row_dev), 1), 1.0, 0.0).astype(BF16)
-    is_low = jnp.broadcast_to(row, (row_dev, HD)) < rows_axis // 2
-
     def take(pieces, buffer, way, child):
         stats = buffer[way, child - 1, :16, :]
         return [
@@ -368,34 +352,73 @@
             for piece in range(2)
         ]
 
-    for child in last[:-1]:
+    swap = pltpu.make_async_remote_copy(
+        src_ref=own_msg,
+        dst_ref=far_msg,
+        send_sem=att_sem.at[0],
+        recv_sem=att_sem.at[1],
+        device_id=(me, across),
+        device_id_type=MESH,
+    )
+
+    def att(pieces):
+        return jnp.concatenate([pieces[0][0], pieces[1][0]], 0).astype(BF16)
+
+    def finish_early():
+        own_msg[:16, :] = packed([stat for _, stat in own])
+        own_msg[16:, :] = o.astype(BF16)
+        swap.start()
+        mine = own
+        for child in last[:-1]:
+            for way in range(2):
+                message(way, child).wait_recv()
+                mine = take(mine, recv, way, child)
+        swap.wait_recv()
+        stats = far_msg[:16, :]
+        far = [
+            (far_msg[16 + piece * half : 16 + (piece + 1) * half, :].astype(F32), unpacked(stats, piece))
+            for piece in range(2)
+        ]
+        for child in last[:-1]:
+            for way in range(2):
+                message_across(way, child).wait_recv()
+                far = take(far, recv_far, way, child)
         for way in range(2):
-            message(way, child).wait_recv()
-            own = take(own, recv, way, child)
-    swap.wait_recv()
-    stats = far_msg[:16, :]
-    far = [
-        (far_msg[16 + piece * half : 16 + (piece + 1) * half, :].astype(F32), unpacked(stats, piece))
-        for piece in range(2)
-    ]
-    for child in last[:-1]:
+            message(way, last[-1]).wait_recv()
+            mine = take(mine, recv, way, last[-1])
         for way in range(2):
-            message_across(way, child).wait_recv()
-            far = take(far, recv_far, way, child)
-    for way in range(2):
-        message(way, last[-1]).wait_recv()
-        own = take(own, recv, way, last[-1])
-    for way in range(2):
-        message_across(way, last[-1]).wait_recv()
-        far = take(far, recv_far, way, last[-1])
-    o = jnp.concatenate([own[0][0], own[1][0]], 0).astype(BF16)
-    o_far = jnp.concatenate([far[0][0], far[1][0]], 0).astype(BF16)
+            message_across(way, last[-1]).wait_recv()
+            far = take(far, recv_far, way, last[-1])
+        att_own[...] = att(mine)
+        att_far[...] = att(far)
+
+    def finish_late():
+        mine = own
+        for child in last:
+            for way in range(2):
+                message(way, child).wait_recv()
+                mine = take(mine, recv, way, child)
+        own_msg[16:, :] = att(mine)
+        own_msg[:16, :] = jnp.zeros((16, HD), BF16)
+        swap.start()
+        att_own[...] = own_msg[16:, :]
+        swap.wait_recv()
+        att_far[...] = far_msg[16:, :]
+
+    place = jnp.zeros((row_dev, row_dev), jnp.int32)
+    for r in range(row_dev):
+        partner = lax.rem(pair_ref[row * row_dev + r], row_dev)
+        place = jnp.where(iota((row_dev, row_dev), 0) == r, partner, place)
+    chosen = jnp.where(place == iota((row_dev, row_dev), 1), 1.0, 0.0).astype(BF16)
+    is_low = jnp.broadcast_to(row, (row_dev, HD)) < rows_axis // 2
+    pl.when(me < EARLY)(finish_early)
+    pl.when(me >= EARLY)(finish_late)
     for head in range(share):
         guide = guide_ref[me * share + head]
         for t in range(steps):
             i = (head * steps + t) * row_dev
-            mine = o[i : i + row_dev].astype(F32)
-            other = jnp.dot(chosen, o_far[i : i + row_dev], preferred_element_type=F32)
+            mine = att_own[i : i + row_dev, :].astype(F32)
+            other = jnp.dot(chosen, att_far[i : i + row_dev, :], preferred_element_type=F32)
             cond = jnp.where(is_low, mine, other)
             uncond = jnp.where(is_low, other, mine)
             mix = uncond + guide * (cond - uncond)
@@ -407,7 +430,7 @@
         for d in PARENT:
             message(way, d).wait_send()
         for d in last:
-            message_across(way, d).wait_send()
+            pl.when(early(way, d))(lambda way=way, d=d: message_across(way, d).wait_send())
 
 
 def local(seq, rows_axis, queries, pk, pv, sk, sv, nk, nv, lengths, pair_of, guidance):
@@ -438,6 +461,8 @@
             pltpu.VMEM((2, max(d for d in PARENT if PARENT[d] == 0), 16 + block, HD), BF16),
             pltpu.VMEM((16 + block, HD), BF16),
             pltpu.VMEM((16 + block, HD), BF16),
+            pltpu.VMEM((block, HD), BF16),
+            pltpu.VMEM((block, HD), BF16),
             pltpu.SemaphoreType.DMA((7,)),
             pltpu.SemaphoreType.DMA((2, hops)),
             pltpu.SemaphoreType.DMA((2, hops)),

time: 42.5 us -> 41 us (0.965)
  Pallas kernels: 40.8 us -> 39.3 us
    pallas_call x1, Pallas kernels: 40.8 us -> 39.3 us  [local(): pl.pallas_call(functools.partial(kernel, seq, rows_axis), out_shape=jax.S...]
where the time goes in v3:
time: 41 us; the launch traced here: 40.7 us
  Pallas kernels  39.3 us (96%)
  local copies, waits for them, and re-layouts  1.42 us (3%)
    pallas_call x1, Pallas kernels, local(): pl.pallas_call(functools.partial(kernel, seq, rows_axis), out_shape=jax.S...  39.3 us
    unnamed x1, local copies, waits for them, and re-layouts  1.42 us

profile of v3, /device:TPU:6, one launch (start us, length us, event | category | flops | bytes accessed | tf_op | source)
XLA Modules:
  0.0 40.7 jit_solution(12757127335005888267)
XLA Ops:
  0.0 39.3 %shard_map.100 = bf16[3,16,512]{2,1,0:T(8,128)(2,1)} custom-call(bf16[3,16,8192]{2,1,0:T(8,128)(2,1)} %q_hbm.1, bf16[1536,512]{1,0:T(8,128)(2,1)} %pk_hbm.1, bf16[1536,512]{1,0:T(8,128)(2,1)} %pv_hbm.1, bf16[16,64,512]{2,1,0:T(8,128)(2,1)} %sk_hbm.1, bf16[16,64,512]{2,1,0:T(8,128)(2,1)} %sv_hbm.1, bf16[3,16,512]{2,1,0:T(8,128)(2,1)} %nk_hbm.1, ...), custom_call_target="tpu_custom_call" | custom-call | tf_op jit(solution)/shard_map/pallas_call | solution.py:445
  39.3 1.4 %copy.12 = bf16[3,16,512]{2,1,0:T(8,128)(2,1)} copy(bf16[3,16,512]{2,1,0:T(8,128)(2,1)} %shard_map.100) | data formatting | bytes 98304

commit v4 on v3

--- a/solution.py
+++ b/solution.py
@@ -105,7 +105,7 @@
 
     barrier = pltpu.get_barrier_semaphore()
     peers = [reach(way, span, row) for span in spans for way in range(2)]
-    peers += [reach(way, span, across) for span in last for way in range(2)] + [(me, across)]
+    peers += [reach(way, span, across) for span in last[-1:] for way in range(2)] + [(me, across)]
     for device in peers:
         pl.semaphore_signal(barrier, inc=1, device_id=device, device_id_type=MESH)
 
@@ -244,7 +244,7 @@
 
     def send_on(way, d):
         message(way, d).start()
-        if PARENT[d] == 0:
+        if d == last[-1]:
             pl.when(early(way, d))(lambda: message_across(way, d).start())
 
     o, lse = partial(lax.rem(me + hops, seq))
@@ -365,24 +365,20 @@
         return jnp.concatenate([pieces[0][0], pieces[1][0]], 0).astype(BF16)
 
     def finish_early():
-        own_msg[:16, :] = packed([stat for _, stat in own])
-        own_msg[16:, :] = o.astype(BF16)
-        swap.start()
         mine = own
         for child in last[:-1]:
             for way in range(2):
                 message(way, child).wait_recv()
                 mine = take(mine, recv, way, child)
+        own_msg[:16, :] = packed([stat for _, stat in mine])
+        own_msg[16:, :] = att(mine)
+        swap.start()
         swap.wait_recv()
         stats = far_msg[:16, :]
         far = [
             (far_msg[16 + piece * half : 16 + (piece + 1) * half, :].astype(F32), unpacked(stats, piece))
             for piece in range(2)
         ]
-        for child in last[:-1]:
-            for way in range(2):
-                message_across(way, child).wait_recv()
-                far = take(far, recv_far, way, child)
         for way in range(2):
             message(way, last[-1]).wait_recv()
             mine = take(mine, recv, way, last[-1])
@@ -429,7 +425,7 @@
     for way in range(2):
         for d in PARENT:
             message(way, d).wait_send()
-        for d in last:
+        for d in last[-1:]:
             pl.when(early(way, d))(lambda way=way, d=d: message_across(way, d).wait_send())
 
 

time: 41 us -> 40.7 us (level)
  no operation moved by 1% of the time
where the time goes in v4:
time: 40.7 us; the launch traced here: 40.5 us
  Pallas kernels  39.1 us (96%)
  local copies, waits for them, and re-layouts  1.42 us (3%)
    pallas_call x1, Pallas kernels, local(): pl.pallas_call(functools.partial(kernel, seq, rows_axis), out_shape=jax.S...  39.1 us
    unnamed x1, local copies, waits for them, and re-layouts  1.42 us

profile of v4, /device:TPU:6, one launch (start us, length us, event | category | flops | bytes accessed | tf_op | source)
XLA Modules:
  0.0 40.5 jit_solution(14721157974485401180)
XLA Ops:
  0.0 39.1 %shard_map.100 = bf16[3,16,512]{2,1,0:T(8,128)(2,1)} custom-call(bf16[3,16,8192]{2,1,0:T(8,128)(2,1)} %q_hbm.1, bf16[1536,512]{1,0:T(8,128)(2,1)} %pk_hbm.1, bf16[1536,512]{1,0:T(8,128)(2,1)} %pv_hbm.1, bf16[16,64,512]{2,1,0:T(8,128)(2,1)} %sk_hbm.1, bf16[16,64,512]{2,1,0:T(8,128)(2,1)} %sv_hbm.1, bf16[3,16,512]{2,1,0:T(8,128)(2,1)} %nk_hbm.1, ...), custom_call_target="tpu_custom_call" | custom-call | tf_op jit(solution)/shard_map/pallas_call | solution.py:441
  39.1 1.4 %copy.12 = bf16[3,16,512]{2,1,0:T(8,128)(2,1)} copy(bf16[3,16,512]{2,1,0:T(8,128)(2,1)} %shard_map.100) | data formatting | bytes 98304

commit v5 on v3

--- a/solution.py
+++ b/solution.py
@@ -422,8 +422,8 @@
             cond = jnp.where(is_low, mine, other)
             uncond = jnp.where(is_low, other, mine)
             mix = uncond + guide * (cond - uncond)
-            norm = jnp.sqrt(jnp.mean(mix * mix, 1, keepdims=True) + 1e-06)
-            out_ref[t, :, head * HD : (head + 1) * HD] = (mix / norm).astype(BF16)
+            factor = lax.rsqrt(jnp.mean(mix * mix, 1, keepdims=True) + 1e-06)
+            out_ref[t, :, head * HD : (head + 1) * HD] = (mix * factor).astype(BF16)
 
     swap.wait_send()
     for way in range(2):

time: 41 us -> 41 us (level)
  no operation moved by 1% of the time
where the time goes in v5:
time: 41 us; the launch traced here: 40.7 us
  Pallas kernels  39.3 us (96%)
  local copies, waits for them, and re-layouts  1.42 us (3%)
    pallas_call x1, Pallas kernels, local(): pl.pallas_call(functools.partial(kernel, seq, rows_axis), out_shape=jax.S...  39.3 us
    unnamed x1, local copies, waits for them, and re-layouts  1.42 us

profile of v5, /device:TPU:6, one launch (start us, length us, event | category | flops | bytes accessed | tf_op | source)
XLA Modules:
  0.0 40.7 jit_solution(12355651941888497968)
XLA Ops:
  0.0 39.3 %shard_map.100 = bf16[3,16,512]{2,1,0:T(8,128)(2,1)} custom-call(bf16[3,16,8192]{2,1,0:T(8,128)(2,1)} %q_hbm.1, bf16[1536,512]{1,0:T(8,128)(2,1)} %pk_hbm.1, bf16[1536,512]{1,0:T(8,128)(2,1)} %pv_hbm.1, bf16[16,64,512]{2,1,0:T(8,128)(2,1)} %sk_hbm.1, bf16[16,64,512]{2,1,0:T(8,128)(2,1)} %sv_hbm.1, bf16[3,16,512]{2,1,0:T(8,128)(2,1)} %nk_hbm.1, ...), custom_call_target="tpu_custom_call" | custom-call | tf_op jit(solution)/shard_map/pallas_call | solution.py:445
  39.3 1.4 %copy.12 = bf16[3,16,512]{2,1,0:T(8,128)(2,1)} copy(bf16[3,16,512]{2,1,0:T(8,128)(2,1)} %shard_map.100) | data formatting | bytes 98304
